TPU v7x, 32 devices: a whole 2x2x4 slice. The times are simulated.
32 devices in a mesh: req: 8 (over y, x, core), tp: 4 (over z).
Axes of the slice: x: 2, y: 2, z: 4, core: 2. Of those that a mesh axis runs over, the one named last changes fastest.
Arguments:
- embeds: bfloat16 [2048, 2048], P(('req', 'tp')), may hold values from -25 to 25
- input_norm_gain: float32 [2048], replicated, may hold values from 0.25 to 1.75
- input_norm_bias: float32 [2048], replicated, may hold values from -3 to 3
- joined_projection_weight: bfloat16 [2048, 6144], P(None, 'tp'), may hold values from -0.125 to 0.125
- joined_projection_bias: float32 [6144], P('tp'), may hold values from -3 to 3
- adapter_down_weight: bfloat16 [4, 2048, 16], replicated, may hold values from -0.125 to 0.125
- adapter_up_weight: bfloat16 [4, 16, 6144], P(None, None, 'tp'), may hold values from -1.5 to 1.5
- attention_out_weight: bfloat16 [2048, 2048], P('tp'), may hold values from -0.125 to 0.125
- attention_out_bias: float32 [2048], replicated, may hold values from -3 to 3
- post_attention_norm_gain: float32 [2048], replicated, may hold values from 0.4 to 1.6
- post_attention_norm_bias: float32 [2048], replicated, may hold values from -3 to 3
- feedforward_up_weight: bfloat16 [2048, 4096], P(None, 'tp'), may hold values from -0.125 to 0.125
- feedforward_up_bias: float32 [4096], P('tp'), may hold values from -3 to 3
- feedforward_down_weight: bfloat16 [4096, 2048], P('tp'), may hold values from -0.09375 to 0.09375
- feedforward_down_bias: float32 [2048], replicated, may hold values from -3 to 3
- stored_keys: bfloat16 [8, 1024, 2048], P('req', None, 'tp'), may hold values from -400 to 400
- stored_values: bfloat16 [8, 1024, 2048], P('req', None, 'tp'), may hold values from -6 to 6
- stored_length: int32 [8], P('req'), may hold values from 2 to 1024, as said below
- tenant_first_request: int32 [3], replicated, may hold values from 1 to 7, as said below
- accept: int32 [2048], P(('req', 'tp')), may hold values 0 or 1
- replacement_token_index: int32 [2048], P('req'), may hold values from 0 to 50175, as said below
- word_embedding_table: bfloat16 [50176, 2048], P('req', 'tp'), may hold values from -6 to 6
Outputs:
- denoised: bfloat16 [2048, 2048], P(('req', 'tp'))
Inputs may be any that keep to these rules, and one draw needn't show every extreme that they name: `stored_length`: one request has exactly 1024 cached positions. `tenant_first_request`: strictly increasing. `replacement_token_index`: of the 256 ids of one index of req, at most 96 lie in the rows o * 6272 to (o + 1) * 6272 - 1 of any one index o of req; one index o receives exactly 96 from every index of req, and every other index receives about equally many.
All inputs are finite; a program needn't handle non-finite values. No bound on the sum of `accept` on one device may be relied on, other than what follows from the above.
Results may differ from a plain program's by a relative error of at most 0.04.
Values may be sent and summed in bfloat16 or wider, within the bound.
A program may use at most 128 MiB of HBM per device.

v0:
```python
import jax
import jax.numpy as jnp
from jax import lax
from jax.sharding import PartitionSpec as P

H = 16
HD = 128
BLK = 256


EPSILON = 1e-05


def layer_norm(residual_state, gain, shift):
    values = residual_state.astype(jnp.float32)
    row_mean = jnp.mean(values, axis=-1, keepdims=True)
    centered = values - row_mean
    variance = jnp.mean(centered * centered, axis=-1, keepdims=True)
    return (centered * lax.rsqrt(variance + EPSILON) * gain + shift).astype(jnp.bfloat16)


def attend(queries, keys_block, values_block, keys_cache, values_cache, length, slopes):
    block_len = queries.shape[0]
    local_heads = queries.shape[1]
    head_size = queries.shape[2]
    score_scale = 1.0 / jnp.sqrt(jnp.float32(head_size))
    block_pos = jnp.arange(block_len)
    query_pos = length + block_pos
    scores = (
        jnp.einsum("qhd,khd->hqk", queries, keys_block, preferred_element_type=jnp.float32)
        * score_scale
    )
    distance = jnp.abs(block_pos[:, None] - block_pos[None, :]).astype(jnp.float32)
    scores = scores - slopes[:, None, None] * distance[None, :, :]
    row_max = jnp.max(scores, axis=-1)
    weights = jnp.exp(scores - row_max[..., None])
    row_total = jnp.sum(weights, axis=-1)
    accum = jnp.einsum(
        "hqk,khd->hqd",
        weights.astype(jnp.bfloat16),
        values_block,
        preferred_element_type=jnp.float32,
    )
    cache_rows = keys_cache.shape[0]
    tile_len = min(512, cache_rows)
    tile_count = (length + tile_len - 1) // tile_len

    def cache_step(index, state_in):
        old_max, old_total, old_accum = state_in
        first_pos = index * tile_len
        key_tile = lax.dynamic_slice_in_dim(keys_cache, first_pos, tile_len, 0).reshape(
            tile_len, local_heads, head_size
        )
        value_tile = lax.dynamic_slice_in_dim(values_cache, first_pos, tile_len, 0).reshape(
            tile_len, local_heads, head_size
        )
        key_pos = first_pos + jnp.arange(tile_len)
        tile_scores = (
            jnp.einsum("qhd,khd->hqk", queries, key_tile, preferred_element_type=jnp.float32)
            * score_scale
        )
        gaps = (query_pos[:, None] - key_pos[None, :]).astype(jnp.float32)
        tile_scores = tile_scores - slopes[:, None, None] * gaps[None, :, :]
        tile_scores = jnp.where((key_pos < length)[None, None, :], tile_scores, -jnp.inf)
        new_max = jnp.maximum(old_max, jnp.max(tile_scores, axis=-1))
        shrink = jnp.exp(old_max - new_max)
        tile_weights = jnp.exp(tile_scores - new_max[..., None])
        new_total = old_total * shrink + jnp.sum(tile_weights, axis=-1)
        new_accum = old_accum * shrink[..., None] + jnp.einsum(
            "hqk,khd->hqd",
            tile_weights.astype(jnp.bfloat16),
            value_tile,
            preferred_element_type=jnp.float32,
        )
        return (new_max, new_total, new_accum)

    row_max, row_total, accum = lax.fori_loop(
        0, tile_count, cache_step, (row_max, row_total, accum)
    )
    context = (accum / row_total[..., None]).astype(jnp.bfloat16)
    return jnp.transpose(context, (1, 0, 2)).reshape(block_len, local_heads * head_size)


def shards(
    embeds,
    input_norm_gain,
    input_norm_bias,
    joined_projection_weight,
    joined_projection_bias,
    adapter_down_weight,
    adapter_up_weight,
    attention_out_weight,
    attention_out_bias,
    post_attention_norm_gain,
    post_attention_norm_bias,
    feedforward_up_weight,
    feedforward_up_bias,
    feedforward_down_weight,
    feedforward_down_bias,
    stored_keys,
    stored_values,
    stored_length,
    tenant_first_request,
    accept,
    replacement_token_index,
    word_embedding_table,
):
    tp_rank = lax.axis_index("tp")
    req_rank = lax.axis_index("req")
    local_heads = joined_projection_weight.shape[1] // (3 * HD)
    requests = stored_keys.shape[0]
    tok_rows = requests * BLK
    share_rows = embeds.shape[0]
    table_rows = word_embedding_table.shape[0]
    head_index = tp_rank * local_heads + jnp.arange(local_heads)
    slopes = jnp.exp2(-8.0 * (head_index + 1).astype(jnp.float32) / H)
    owned = req_rank * requests + jnp.arange(requests)
    tenant_index = jnp.sum(
        (owned[:, None] >= tenant_first_request[None, :]).astype(jnp.int32), axis=1
    )
    adapter_inputs = [
        lax.dynamic_index_in_dim(adapter_down_weight, tenant_index[0], 0, keepdims=False)
    ]
    adapter_outputs = [
        lax.dynamic_index_in_dim(adapter_up_weight, tenant_index[0], 0, keepdims=False)
    ]

    def project(shard_rows):
        joined = jnp.dot(shard_rows, joined_projection_weight, preferred_element_type=jnp.float32)
        row_request = jnp.arange(shard_rows.shape[0]) // BLK
        low_rank_rows = jnp.dot(
            shard_rows, adapter_inputs[0], preferred_element_type=jnp.float32
        ).astype(jnp.bfloat16)
        lifted = jnp.dot(low_rank_rows, adapter_outputs[0], preferred_element_type=jnp.float32)
        joined = joined + jnp.where((row_request == 0)[:, None], lifted, 0.0)
        return (joined + joined_projection_bias).astype(jnp.bfloat16)

    def expand(shard_rows):
        inner = (
            jnp.dot(shard_rows, feedforward_up_weight, preferred_element_type=jnp.float32)
            + feedforward_up_bias
        )
        return jax.nn.gelu(inner, approximate=True).astype(jnp.bfloat16)

    def share_sum(left, right):
        partial_sum = jnp.dot(left, right, preferred_element_type=jnp.float32)
        summed = lax.psum(partial_sum.astype(jnp.bfloat16), "tp").astype(jnp.float32)
        return lax.dynamic_slice_in_dim(summed, tp_rank * share_rows, share_rows, 0)

    def run_layer_pass(residual_state):
        normed = layer_norm(residual_state, input_norm_gain, input_norm_bias)
        joined = project(lax.all_gather(normed, "tp", axis=0, tiled=True))
        heads_view = joined.reshape(tok_rows, local_heads, 3, HD)
        contexts = attend(
            heads_view[:, :, 0],
            heads_view[:, :, 1],
            heads_view[:, :, 2],
            stored_keys[0],
            stored_values[0],
            stored_length[0],
            slopes,
        )
        attended = (
            residual_state.astype(jnp.float32)
            + share_sum(contexts, attention_out_weight)
            + attention_out_bias
        ).astype(jnp.bfloat16)
        post = layer_norm(attended, post_attention_norm_gain, post_attention_norm_bias)
        hidden = expand(lax.all_gather(post, "tp", axis=0, tiled=True))
        return (
            attended.astype(jnp.float32)
            + share_sum(hidden, feedforward_down_weight)
            + feedforward_down_bias
        ).astype(jnp.bfloat16)

    all_ids = lax.all_gather(replacement_token_index, "req", axis=0, tiled=True)
    local_index = all_ids - req_rank * table_rows
    inside = (local_index >= 0) & (local_index < table_rows)
    found = jnp.take(word_embedding_table, jnp.clip(local_index, 0, table_rows - 1), axis=0)
    columns = lax.psum_scatter(
        jnp.where(inside[:, None], found.astype(jnp.float32), 0.0).astype(jnp.bfloat16),
        "req",
        scatter_dimension=0,
        tiled=True,
    )
    replacement = lax.all_to_all(columns, "tp", split_axis=0, concat_axis=1, tiled=True)
    first = run_layer_pass(embeds)
    second_in = jnp.where((accept == 1)[:, None], replacement, first)
    return run_layer_pass(second_in)


def solution(mesh):
    in_specs = (
        P(("req", "tp"), None),
        P(),
        P(),
        P(None, "tp"),
        P("tp"),
        P(),
        P(None, None, "tp"),
        P("tp", None),
        P(),
        P(),
        P(),
        P(None, "tp"),
        P("tp"),
        P("tp", None),
        P(),
        P("req", None, "tp"),
        P("req", None, "tp"),
        P("req"),
        P(),
        P(("req", "tp")),
        P("req"),
        P("req", "tp"),
    )
    out_specs = P(("req", "tp"), None)
    return jax.shard_map(shards, mesh=mesh, in_specs=in_specs, out_specs=out_specs, check_vma=False)
```

profile of v0, /device:TPU:0, one launch (start us, length us, event | category | flops | bytes accessed | tf_op | source)
XLA Modules:
  0.0 433.9 jit_solution(809088786829762818)
XLA Ops:
  9.8 1.8 fusion.67
  16.5 2.3 copy.68
  19.5 23.0 %all-gather.6.cloned.1.call-done = bf16[256,2048]{1,0:T(8,128)(2,1)} async-done(((bf16[64,2048]{1,0:T(8,128)(2,1)}), bf16[256,2048]{1,0:T(8,128)(2,1)}) %all-gather.6.cloned.1.call-update) | async-done | bytes 1048592 | tf_op jit(solution)/shard_map/all_gather | solution.py:152
  42.5 6.1 %fusion.131 = f32[256,1536]{1,0:T(8,128)} fusion(bf16[256,2048]{1,0:T(8,128)(2,1)} %all-gather.6.cloned.1.call-done, bf16[2048,1536]{1,0:T(8,128)(2,1)} %param.29), kind=kOutput, calls=%fused_computation.196 | convolution fusion | flops 1610612736 | bytes 8912896 | tf_op jit(solution)/shard_map/dot_general | solution.py:129
  48.6 3.8 fusion.23
  52.4 2.3 copy.62
  56.1 2.1 fusion.78
  60.2 5.2 %while.32 = (s32[]{:T(128)}, f32[4,256]{1,0:T(4,128)S(1)}, f32[4,256]{1,0:T(4,128)S(1)}, f32[4,256,128]{2,1,0:T(8,128)}, s32[]{:T(128)}, /*index=5*/s32[]{:T(128...) while((s32[]{:T(128)}, f32[4,256]{1,0:T(4,128)S(1)}, ...), condition=%wide.region_9.10_spmd.clone.clone, body=%wide.region_6.9_spmd.clone.clone.sunk | while | flops 273682176 | bytes 17112384 | solution.py:77
  65.3 2.1 copy.69
  68.5 1.8 convolution_convert_fusion.1
  70.4 56.6 %all-reduce.5.cloned.1.call-done = bf16[256,2048]{1,0:T(8,128)(2,1)} async-done(((bf16[256,2048]{1,0:T(8,128)(2,1)}), bf16[256,2048]{1,0:T(8,128)(2,1)}) %all-reduce.5.cloned.1.call-update) | async-done | bytes 1048592 | tf_op jit(solution)/shard_map/psum | solution.py:147
  129.8 8.9 %all-gather = s32[8,1,256]{2,1,0:T(1,128)S(1)} all-gather(s32[1,1,256]{2,1,0:T(1,128)S(1)} %bitcast.137), channel_id=1, replica_groups=mesh['req'=8,'tp'=4] {'req'}, dimensions={0}, use_global_device_ids=true | all-gather | bytes 9216 | tf_op jit(solution)/shard_map/all_gather | solution.py:176
  138.7 12.9 %gather_fusion = bf16[2048,512]{1,0:T(8,128)(2,1)} fusion(bf16[6272,512]{1,0:T(8,128)(2,1)} %param.47, s32[2048]{0:T(1024)S(1)} %fusion.107), kind=kCustom, calls=%fused_computation | custom fusion | bytes 4202496 | tf_op jit(solution)/shard_map/jit(_take)/gather | solution.py:179
  151.6 3.0 select_convert_fusion
  154.7 2.5 all-gather.8.cloned.1.call-done
  157.2 7.7 %convolution_convert_fusion.3 = bf16[256,2048]{1,0:T(8,128)(2,1)} fusion(bf16[1024,2048]{1,0:T(8,128)(2,1)} %param.39, bf16[256,2048]{1,0:T(8,128)(2,1)} %all-gather.8.cloned.1.call-done, bf16[2048,1024]{1,0:T(8,128)(2,1)} %param.37, f32[1024]{0:T(1024)S(1)} %copy-done.18), kind=kOutput, calls=%fused_computation.49 | convolution fusion | flops 2150629376 | bytes 10489856 | tf_op jit(solution)/shard_map/dot_general | solution.py:146
  164.9 29.5 %reduce-scatter.2.cloned.1.call-done = bf16[256,512]{1,0:T(8,128)(2,1)} async-done(((bf16[2048,512]{1,0:T(8,128)(2,1)}), bf16[256,512]{1,0:T(8,128)(2,1)}) %reduce-scatter.2.cloned.1.call-update) | async-done | bytes 262160 | tf_op jit(solution)/shard_map/reduce_scatter | solution.py:180
  194.4 4.6 %all-to-all-start = ((bf16[4,64,512]{2,1,0:T(8,128)(2,1)}), bf16[4,64,512]{2,1,0:T(8,128)(2,1)S(1)}, u32[]{:S(2)}, u32[]{:S(2)}) async-start(bf16[4,64,512]{2,1,0:T(8,128)(2,1)} %bitcast.134), calls=%async_computation.1 | async-start | bytes 524288 | tf_op jit(solution)/shard_map/all_to_all | solution.py:186
  199.0 16.4 %all-to-all-done = bf16[4,64,512]{2,1,0:T(8,128)(2,1)S(1)} async-done(((bf16[4,64,512]{2,1,0:T(8,128)(2,1)}), bf16[4,64,512]{2,1,0:T(8,128)(2,1)S(1)}, u32[]{:S(2)}, u32[]{:S(2)}) %all-to-all-start) | async-done | bytes 262176 | tf_op jit(solution)/shard_map/all_to_all | solution.py:186
  216.1 6.2 %all-reduce.7.cloned.1.call-done = bf16[256,2048]{1,0:T(8,128)(2,1)} async-done(((bf16[256,2048]{1,0:T(8,128)(2,1)}), bf16[256,2048]{1,0:T(8,128)(2,1)}) %all-reduce.7.cloned.1.call-update) | async-done | bytes 1048592 | tf_op jit(solution)/shard_map/psum | solution.py:147
  224.9 26.8 %all-gather.10.cloned.1.call-done = bf16[256,2048]{1,0:T(8,128)(2,1)} async-done(((bf16[64,2048]{1,0:T(8,128)(2,1)}), bf16[256,2048]{1,0:T(8,128)(2,1)}) %all-gather.10.cloned.1.call-update) | async-done | bytes 1048592 | tf_op jit(solution)/shard_map/all_gather | solution.py:152
  251.8 6.1 %fusion.132 = f32[256,1536]{1,0:T(8,128)} fusion(bf16[256,2048]{1,0:T(8,128)(2,1)} %all-gather.10.cloned.1.call-done, bf16[2048,1536]{1,0:T(8,128)(2,1)} %param.29), kind=kOutput, calls=%fused_computation.197 | convolution fusion | flops 1610612736 | bytes 8912896 | tf_op jit(solution)/shard_map/dot_general | solution.py:129
  257.8 3.8 fusion.22
  261.7 2.3 copy.70
  265.4 2.1 fusion.76
  269.4 1.8 copy.87
  271.2 5.2 %while.33 = (s32[]{:T(128)}, f32[4,256]{1,0:T(4,128)S(1)}, f32[4,256]{1,0:T(4,128)S(1)}, f32[4,256,128]{2,1,0:T(8,128)}, s32[]{:T(128)}, /*index=5*/s32[]{:T(128...) while((s32[]{:T(128)}, f32[4,256]{1,0:T(4,128)S(1)}, ...), condition=%wide.region_21.22_spmd.clone.clone, body=%wide.region_18.21_spmd.clone.clone.sunk | while | flops 273682176 | bytes 17112384 | solution.py:77
  277.6 1.8 convolution_convert_fusion
  279.5 56.6 %all-reduce.9.cloned.1.call-done = bf16[256,2048]{1,0:T(8,128)(2,1)} async-done(((bf16[256,2048]{1,0:T(8,128)(2,1)}), bf16[256,2048]{1,0:T(8,128)(2,1)}) %all-reduce.9.cloned.1.call-update) | async-done | bytes 1048592 | tf_op jit(solution)/shard_map/psum | solution.py:147
  338.4 27.4 %all-gather.12.cloned.1.call-done = bf16[256,2048]{1,0:T(8,128)(2,1)} async-done(((bf16[64,2048]{1,0:T(8,128)(2,1)}), bf16[256,2048]{1,0:T(8,128)(2,1)}) %all-gather.12.cloned.1.call-update) | async-done | bytes 1048592 | tf_op jit(solution)/shard_map/all_gather | solution.py:169
  365.8 7.4 %convolution_convert_fusion.2 = bf16[256,2048]{1,0:T(8,128)(2,1)} fusion(bf16[1024,2048]{1,0:T(8,128)(2,1)} %param.39, bf16[256,2048]{1,0:T(8,128)(2,1)} %all-gather.12.cloned.1.call-done, bf16[2048,1024]{1,0:T(8,128)(2,1)} %param.37, f32[1024]{0:T(1024)S(1)} %copy-done.18), kind=kOutput, calls=%fused_computation.48 | convolution fusion | flops 2150629376 | bytes 10489856 | tf_op jit(solution)/shard_map/dot_general | solution.py:146
  373.2 51.5 %all-reduce.11.cloned.1.call-done = bf16[256,2048]{1,0:T(8,128)(2,1)} async-done(((bf16[256,2048]{1,0:T(8,128)(2,1)}), bf16[256,2048]{1,0:T(8,128)(2,1)}) %all-reduce.11.cloned.1.call-update) | async-done | bytes 1048592 | tf_op jit(solution)/shard_map/psum | solution.py:147
  (124 shorter events, 34.9 us)
Async XLA Ops:
  7.4 61.1 %copy-start = (bf16[512,2048]{1,0:T(8,128)(2,1)S(1)}, bf16[512,2048]{1,0:T(8,128)(2,1)}, u32[]{:S(2)}) copy-start(bf16[512,2048]{1,0:T(8,128)(2,1)} %param.33) | copy-start | bytes 6291460
  7.4 35.1 %all-gather.6.cloned.1.call-start = ((), (), s32[]{:S(2)}) async-start(), calls=%async_computation.3 | async-start | bytes 1310720 | tf_op jit(solution)/shard_map/all_gather | solution.py:152
  11.7 115.3 %all-reduce.5.cloned.1.call-start = ((), (), s32[]{:S(2)}) async-start(), calls=%async_computation.4 | async-start | bytes 2097152 | tf_op jit(solution)/shard_map/psum | solution.py:147
  19.5 35.2 %copy-start.7 = (f32[256,256]{0,1:T(8,128)}, f32[256,256]{0,1:T(8,128)S(1)}, u32[]{:S(2)}) copy-start(f32[256,256]{0,1:T(8,128)S(1)} %abs_convert_fusion) | copy-start | bytes 786436
  19.5 29.0 %copy-start.12 = (f32[1536]{0:T(1024)S(1)}, f32[1536]{0:T(1024)}, u32[]{:S(2)}) copy-start(f32[1536]{0:T(1024)} %param.30) | copy-start | bytes 18436
  60.2 2.7 copy-start.9
  62.8 1.0 copy-start.1
  64.5 0.8 copy-start.2
  68.5 58.5 %copy-start.6 = (bf16[64,2048]{1,0:T(8,128)(2,1)S(1)}, bf16[64,2048]{1,0:T(8,128)(2,1)}, u32[]{:S(2)}) copy-start(bf16[64,2048]{1,0:T(8,128)(2,1)} %param.26) | copy-start | bytes 786436
  68.5 58.5 %copy-start.13 = (f32[2048]{0:T(1024)S(1)}, f32[2048]{0:T(1024)}, u32[]{:S(2)}) copy-start(f32[2048]{0:T(1024)} %param.34) | copy-start | bytes 24580
  68.5 60.3 %copy-start.14 = (f32[2048]{0:T(1024)S(1)}, f32[2048]{0:T(1024)}, u32[]{:S(2)}) copy-start(f32[2048]{0:T(1024)} %param.36) | copy-start | bytes 24580
  68.5 60.3 %copy-start.15 = (f32[2048]{0:T(1024)S(1)}, f32[2048]{0:T(1024)}, u32[]{:S(2)}) copy-start(f32[2048]{0:T(1024)} %param.35) | copy-start | bytes 24580
  70.3 59.5 %copy-start.17 = (s32[256]{0:T(256)S(1)}, s32[256]{0:T(256)}, u32[]{:S(2)}) copy-start(s32[256]{0:T(256)} %param.46) | copy-start | bytes 3076
  70.3 86.9 %all-gather.8.cloned.1.call-start = ((), (), s32[]{:S(2)}) async-start(), calls=%async_computation.5 | async-start | bytes 1310720 | tf_op jit(solution)/shard_map/all_gather | solution.py:169
  128.1 0.7 copy-start.5
  129.7 64.7 %reduce-scatter.2.cloned.1.call-start = ((), (), s32[]{:S(2)}) async-start(), calls=%async_computation.2 | async-start | bytes 2359296 | tf_op jit(solution)/shard_map/reduce_scatter | solution.py:180
  154.6 2.6 copy-start.18
  154.6 44.4 %copy-start.19 = (s32[64]{0:T(128)S(1)}, s32[64]{0:T(128)}, u32[]{:S(2)}) copy-start(s32[64]{0:T(128)} %param.45) | copy-start | bytes 772
  154.6 67.7 %all-reduce.7.cloned.1.call-start = ((), (), s32[]{:S(2)}) async-start(), calls=%async_computation.6 | async-start | bytes 2097152 | tf_op jit(solution)/shard_map/psum | solution.py:147
  164.9 57.5 %copy-start.16 = (f32[2048]{0:T(1024)S(1)}, f32[2048]{0:T(1024)}, u32[]{:S(2)}) copy-start(f32[2048]{0:T(1024)} %param.40) | copy-start | bytes 24580
  164.9 59.1 %copy-start.10 = (f32[2048]{0:T(1024)S(1)}, f32[2048]{0:T(1024)}, u32[]{:S(2)}) copy-start(f32[2048]{0:T(1024)} %param.28) | copy-start | bytes 24580
  164.9 59.1 %copy-start.11 = (f32[2048]{0:T(1024)S(1)}, f32[2048]{0:T(1024)}, u32[]{:S(2)}) copy-start(f32[2048]{0:T(1024)} %param.27) | copy-start | bytes 24580
  194.4 21.0 %all-to-all-start = ((bf16[4,64,512]{2,1,0:T(8,128)(2,1)}), bf16[4,64,512]{2,1,0:T(8,128)(2,1)S(1)}, u32[]{:S(2)}, u32[]{:S(2)}) async-start(bf16[4,64,512]{2,1,0:T(8,128)(2,1)} %bitcast.134), calls=%async_computation.1 | async-start | bytes 524288 | tf_op jit(solution)/shard_map/all_to_all | solution.py:186
  199.0 52.8 %all-gather.10.cloned.1.call-start = ((), (), s32[]{:S(2)}) async-start(), calls=%async_computation.7 | async-start | bytes 1310720 | tf_op jit(solution)/shard_map/all_gather | solution.py:152
  224.9 111.2 %all-reduce.9.cloned.1.call-start = ((), (), s32[]{:S(2)}) async-start(), calls=%async_computation.8 | async-start | bytes 2097152 | tf_op jit(solution)/shard_map/psum | solution.py:147
  271.2 2.7 copy-start.8
  273.8 1.0 copy-start.3
  275.5 0.8 copy-start.4
  279.4 86.4 %all-gather.12.cloned.1.call-start = ((), (), s32[]{:S(2)}) async-start(), calls=%async_computation.9 | async-start | bytes 1310720 | tf_op jit(solution)/shard_map/all_gather | solution.py:169
  338.4 86.3 %all-reduce.11.cloned.1.call-start = ((), (), s32[]{:S(2)}) async-start(), calls=%async_computation.10 | async-start | bytes 2097152 | tf_op jit(solution)/shard_map/psum | solution.py:147
Sparse Core Ops, SparseCore 0:
  11.8 30.6 all-gather.5
  70.4 56.4 all-reduce.4
  129.8 27.3 all-gather.7
  165.0 57.2 all-reduce.6
  225.0 26.7 all-gather.9
  279.5 56.4 all-reduce.8
  338.5 27.3 all-gather.11
  373.3 51.2 all-reduce.10
Sparse Core Ops, SparseCore 1:
  154.7 39.7 reduce-scatter.1
where the time goes:
time: 433 us; the launch traced here: 434 us
  waiting for transfers between devices  297 us (69%)
  matrix products  48.1 us (11%)
  local copies, waits for them, and re-layouts  35 us (8%)
  other arithmetic  22.4 us (5%)
  between operations  17.8 us (4%)
  blocking collectives  8.86 us (2%)
  starting transfers between devices  4.9 us (1%)
    psum x4, waiting for transfers between devices, share_sum(): lax.psum(partial_sum.astype(jnp.bfloat16), 'tp').astype(jnp.float32)  171 us
    all_gather x2, waiting for transfers between devices, run_layer_pass(): joined = project(lax.all_gather(normed, 'tp', axis=0, tiled=True))  49.8 us
    all_gather x2, waiting for transfers between devices, run_layer_pass(): hidden = expand(lax.all_gather(post, 'tp', axis=0, tiled=True))  29.9 us
    reduce_scatter x1, waiting for transfers between devices, shards(): lax.psum_scatter(jnp.where(inside[:, None], found.astype(jnp.float32), 0....  29.5 us
    dot_general x4, matrix products, share_sum(): partial_sum = jnp.dot(left, right, preferred_element_type=jnp.float32)  18.6 us
    all_to_all x1, waiting for transfers between devices, shards(): lax.all_to_all(columns, 'tp', split_axis=0, concat_axis=1, tiled=True)  16.4 us
    gather x1, local copies, waits for them, and re-layouts, shards(): jnp.take(word_embedding_table, jnp.clip(local_index, 0, table_rows - 1),...  12.9 us
    dot_general x2, matrix products, project(): jnp.dot(shard_rows, joined_projection_weight, preferred_element_type=jnp....  12.1 us
  transfers between devices with their start and end apart: 10, of which 10 were waited for; matrix products, arithmetic and copies ran while one was open for 7% of the time, Pallas kernels for 0%

commit v1 on v0

v1 whole, which is shorter than its diff:
```python
import functools

import jax
import jax.numpy as jnp
from jax import lax
from jax.experimental import pallas as pl
from jax.experimental.pallas import tpu as pltpu
from jax.sharding import PartitionSpec as P

H = 16
HD = 128
BLK = 256
EPSILON = 1e-05
F32 = jnp.float32
BF16 = jnp.bfloat16


def norm_rows(values, gain, shift):
    mean = jnp.mean(values, axis=-1, keepdims=True)
    centered = values - mean
    variance = jnp.mean(centered * centered, axis=-1, keepdims=True)
    return (centered * lax.rsqrt(variance + EPSILON) * gain + shift).astype(BF16)


def layer_kernel(
    n,
    rows,
    heads,
    length_ref,
    x_ref,
    in_gain,
    in_shift,
    wq_hbm,
    bq_ref,
    ad_ref,
    au_ref,
    wo_hbm,
    bo_ref,
    post_gain,
    post_shift,
    wu_hbm,
    bu_ref,
    wd_hbm,
    bd_ref,
    kc_hbm,
    vc_hbm,
    out_ref,
    wq,
    wo,
    wu,
    wd,
    kc,
    vc,
    gat_a,
    gat_b,
    part_a,
    part_b,
    from_left_a,
    from_right_a,
    from_left_b,
    from_right_b,
    qkv,
    ctx,
    hid,
    attended,
    load_sem,
    gat_send_right,
    gat_send_left,
    gat_recv,
    sum_send,
    sum_recv_left,
    sum_recv_right,
):
    me = lax.axis_index("tp")
    loads = [
        pltpu.make_async_copy(source, target, load_sem.at[index])
        for index, (source, target) in enumerate(
            ((wq_hbm, wq), (kc_hbm, kc), (vc_hbm, vc), (wo_hbm, wo), (wu_hbm, wu), (wd_hbm, wd))
        )
    ]
    for load in loads:
        load.start()
    has_left = me > 0
    has_right = me < n - 1

    barrier = pltpu.get_barrier_semaphore()

    @pl.when(has_left)
    def _():
        pl.semaphore_signal(
            barrier, inc=1, device_id={"tp": me - 1}, device_id_type=pl.DeviceIdType.MESH
        )

    @pl.when(has_right)
    def _():
        pl.semaphore_signal(
            barrier, inc=1, device_id={"tp": me + 1}, device_id_type=pl.DeviceIdType.MESH
        )

    def chunk(index):
        return pl.ds(pl.multiple_of(index * rows, rows), rows)

    gat_a[chunk(me), :] = norm_rows(x_ref[...].astype(F32), in_gain[...], in_shift[...])

    pl.semaphore_wait(barrier, has_left.astype(jnp.int32) + has_right.astype(jnp.int32))

    def gather_copy(which, buffer, index, step):
        sends = gat_send_right if step > 0 else gat_send_left
        return pltpu.make_async_remote_copy(
            src_ref=buffer.at[chunk(index), :],
            dst_ref=buffer.at[chunk(index), :],
            send_sem=sends.at[which, index],
            recv_sem=gat_recv.at[which, index],
            device_id={"tp": me + step},
            device_id_type=pl.DeviceIdType.MESH,
        )

    def gather(which, buffer):
        @pl.when(has_right)
        def _():
            gather_copy(which, buffer, me, 1).start()

        @pl.when(has_left)
        def _():
            gather_copy(which, buffer, me, -1).start()

        for k in range(1, n):

            @pl.when(me - k >= 0)
            def _():
                gather_copy(which, buffer, me - k, 1).wait_recv()

                @pl.when(has_right)
                def _():
                    gather_copy(which, buffer, me - k, 1).start()

            @pl.when(me + k <= n - 1)
            def _():
                gather_copy(which, buffer, me + k, -1).wait_recv()

                @pl.when(has_left)
                def _():
                    gather_copy(which, buffer, me + k, -1).start()

    def gather_end(which, buffer):
        for k in range(n):

            @pl.when((me - k >= 0) & has_right)
            def _():
                gather_copy(which, buffer, me - k, 1).wait_send()

            @pl.when((me + k <= n - 1) & has_left)
            def _():
                gather_copy(which, buffer, me + k, -1).wait_send()

    def sum_copy(which, part, landing, index, step):
        recvs = sum_recv_left if step > 0 else sum_recv_right
        return pltpu.make_async_remote_copy(
            src_ref=part.at[chunk(index), :],
            dst_ref=landing.at[chunk(index), :],
            send_sem=sum_send.at[which, index],
            recv_sem=recvs.at[which, index],
            device_id={"tp": me + step},
            device_id_type=pl.DeviceIdType.MESH,
        )

    def add_in(part, landing, index):
        part[chunk(index), :] = (
            part[chunk(index), :].astype(F32) + landing[chunk(index), :].astype(F32)
        ).astype(BF16)

    def sum_over(which, part, from_left, from_right):
        for k in range(n - 1):
            right_index = n - 1 - k
            left_index = k

            @pl.when(right_index > me)
            def _():
                @pl.when(has_left)
                def _():
                    sum_copy(which, part, from_left, right_index, 1).wait_recv()
                    add_in(part, from_left, right_index)

                sum_copy(which, part, from_left, right_index, 1).start()

            @pl.when(left_index < me)
            def _():
                @pl.when(has_right)
                def _():
                    sum_copy(which, part, from_right, left_index, -1).wait_recv()
                    add_in(part, from_right, left_index)

                sum_copy(which, part, from_right, left_index, -1).start()

        @pl.when(has_left)
        def _():
            sum_copy(which, part, from_left, me, 1).wait_recv()
            add_in(part, from_left, me)

        @pl.when(has_right)
        def _():
            sum_copy(which, part, from_right, me, -1).wait_recv()
            add_in(part, from_right, me)

    def sum_end(which, part, from_left, from_right):
        for k in range(n):

            @pl.when(k > me)
            def _():
                sum_copy(which, part, from_left, k, 1).wait_send()

            @pl.when(k < me)
            def _():
                sum_copy(which, part, from_right, k, -1).wait_send()

    def columns(index, width):
        return pl.ds(pl.multiple_of(index * width, width), width)

    gather(0, gat_a)
    loads[0].wait()
    low = jnp.dot(gat_a[...], ad_ref[...], preferred_element_type=F32).astype(BF16)

    @pl.loop(0, wq.shape[1] // 256)
    def _(tile):
        cols = columns(tile, 256)
        joined = jnp.dot(gat_a[...], wq[:, cols], preferred_element_type=F32)
        joined = joined + jnp.dot(low, au_ref[:, cols], preferred_element_type=F32)
        qkv[:, cols] = (joined + bq_ref[:, cols]).astype(BF16)

    loads[1].wait()
    loads[2].wait()
    length = length_ref[0]
    cache_rows = kc.shape[0]
    block = qkv.shape[0]
    scale = HD**-0.5

    @pl.loop(0, heads)
    def _(head):
        exponent = jnp.zeros((1, 1), F32) + (me * heads + head + 1).astype(F32) * (-8.0 / H)
        slope = jnp.exp2(exponent)
        query = qkv[:, columns(head * 3, HD)]
        key = qkv[:, columns(head * 3 + 1, HD)]
        value = qkv[:, columns(head * 3 + 2, HD)]
        contract = (((1,), (1,)), ((), ()))
        block_scores = lax.dot_general(query, key, contract, preferred_element_type=F32) * scale
        q_pos = lax.broadcasted_iota(jnp.int32, (block, 1), 0)
        k_pos = lax.broadcasted_iota(jnp.int32, (1, block), 1)
        block_scores = block_scores - slope * jnp.abs(q_pos - k_pos).astype(F32)
        cache_scores = (
            lax.dot_general(query, kc[:, columns(head, HD)], contract, preferred_element_type=F32)
            * scale
        )
        c_pos = lax.broadcasted_iota(jnp.int32, (1, cache_rows), 1)
        cache_scores = cache_scores - slope * (q_pos + length - c_pos).astype(F32)
        cache_scores = jnp.where(c_pos < length, cache_scores, -jnp.inf)
        top = jnp.maximum(
            jnp.max(block_scores, axis=-1, keepdims=True),
            jnp.max(cache_scores, axis=-1, keepdims=True),
        )
        block_weights = jnp.exp(block_scores - top)
        cache_weights = jnp.exp(cache_scores - top)
        total = jnp.sum(block_weights, axis=-1, keepdims=True) + jnp.sum(
            cache_weights, axis=-1, keepdims=True
        )
        mixed = jnp.dot(block_weights.astype(BF16), value, preferred_element_type=F32)
        mixed = mixed + jnp.dot(
            cache_weights.astype(BF16), vc[:, columns(head, HD)], preferred_element_type=F32
        )
        ctx[:, columns(head, HD)] = (mixed / total).astype(BF16)

    loads[3].wait()

    @pl.loop(0, wo.shape[1] // 256)
    def _(tile):
        cols = columns(tile, 256)
        part_a[:, cols] = jnp.dot(ctx[...], wo[:, cols], preferred_element_type=F32).astype(BF16)

    sum_over(0, part_a, from_left_a, from_right_a)
    attended[...] = (
        x_ref[...].astype(F32) + part_a[chunk(me), :].astype(F32) + bo_ref[...]
    ).astype(BF16)
    gat_b[chunk(me), :] = norm_rows(attended[...].astype(F32), post_gain[...], post_shift[...])
    gather(1, gat_b)
    loads[4].wait()

    @pl.loop(0, wu.shape[1] // 256)
    def _(tile):
        cols = columns(tile, 256)
        inner = jnp.dot(gat_b[...], wu[:, cols], preferred_element_type=F32) + bu_ref[:, cols]
        hid[:, cols] = jax.nn.gelu(inner, approximate=True).astype(BF16)

    loads[5].wait()

    @pl.loop(0, wd.shape[1] // 256)
    def _(tile):
        cols = columns(tile, 256)
        part_b[:, cols] = jnp.dot(hid[...], wd[:, cols], preferred_element_type=F32).astype(BF16)

    sum_over(1, part_b, from_left_b, from_right_b)
    out_ref[...] = (
        attended[...].astype(F32) + part_b[chunk(me), :].astype(F32) + bd_ref[...]
    ).astype(BF16)
    gather_end(0, gat_a)
    sum_end(0, part_a, from_left_a, from_right_a)
    gather_end(1, gat_b)
    sum_end(1, part_b, from_left_b, from_right_b)


def layer_call(n, x, length, weights):
    rows, width = x.shape
    wq, wo, wu, wd, kc, vc = weights[2], weights[6], weights[10], weights[12], weights[14], weights[15]
    heads = wo.shape[0] // HD
    block = n * rows
    vmem = pl.BlockSpec(memory_space=pltpu.VMEM)
    hbm = pl.BlockSpec(memory_space=pl.ANY)
    smem = pl.BlockSpec(memory_space=pltpu.SMEM)
    in_hbm = (2, 6, 10, 12, 14, 15)
    specs = [smem, vmem] + [hbm if i in in_hbm else vmem for i in range(len(weights))]
    full = pltpu.VMEM((block, width), BF16)
    dma = pltpu.SemaphoreType.DMA
    return pl.pallas_call(
        functools.partial(layer_kernel, n, rows, heads),
        out_shape=jax.ShapeDtypeStruct((rows, width), BF16),
        in_specs=specs,
        out_specs=vmem,
        scratch_shapes=[pltpu.VMEM(a.shape, BF16) for a in (wq, wo, wu, wd, kc, vc)]
        + [full] * 8
        + [
            pltpu.VMEM((block, wq.shape[1]), BF16),
            pltpu.VMEM((block, wo.shape[0]), BF16),
            pltpu.VMEM((block, wu.shape[1]), BF16),
            pltpu.VMEM((rows, width), BF16),
            dma((6,)),
        ]
        + [dma((2, n))] * 6,
        compiler_params=pltpu.CompilerParams(
            collective_id=0, has_side_effects=True, vmem_limit_bytes=52 * 2**20
        ),
        cost_estimate=pl.CostEstimate(
            flops=9_000_000_000, bytes_accessed=20_000_000, transcendentals=1_500_000
        ),
        name="layer_pass",
    )(length, x, *weights)


def shards(
    embeds,
    input_norm_gain,
    input_norm_bias,
    joined_projection_weight,
    joined_projection_bias,
    adapter_down_weight,
    adapter_up_weight,
    attention_out_weight,
    attention_out_bias,
    post_attention_norm_gain,
    post_attention_norm_bias,
    feedforward_up_weight,
    feedforward_up_bias,
    feedforward_down_weight,
    feedforward_down_bias,
    stored_keys,
    stored_values,
    stored_length,
    tenant_first_request,
    accept,
    replacement_token_index,
    word_embedding_table,
):
    n = lax.axis_size("tp")
    req_rank = lax.axis_index("req")
    table_rows = word_embedding_table.shape[0]
    tenant = jnp.sum((req_rank >= tenant_first_request).astype(jnp.int32))
    weights = (
        input_norm_gain[None],
        input_norm_bias[None],
        joined_projection_weight,
        joined_projection_bias[None],
        lax.dynamic_index_in_dim(adapter_down_weight, tenant, 0, keepdims=False),
        lax.dynamic_index_in_dim(adapter_up_weight, tenant, 0, keepdims=False),
        attention_out_weight,
        attention_out_bias[None],
        post_attention_norm_gain[None],
        post_attention_norm_bias[None],
        feedforward_up_weight,
        feedforward_up_bias[None],
        feedforward_down_weight,
        feedforward_down_bias[None],
        stored_keys[0],
        stored_values[0],
    )

    all_ids = lax.all_gather(replacement_token_index, "req", axis=0, tiled=True)
    local_index = all_ids - req_rank * table_rows
    inside = (local_index >= 0) & (local_index < table_rows)
    found = jnp.take(word_embedding_table, jnp.clip(local_index, 0, table_rows - 1), axis=0)
    found = jnp.where(inside[:, None], found.astype(F32), 0.0).astype(BF16)
    columns = lax.psum_scatter(found, "req", scatter_dimension=0, tiled=True)
    replacement = lax.all_to_all(columns, "tp", split_axis=0, concat_axis=1, tiled=True)
    first = layer_call(n, embeds, stored_length, weights)
    second_in = jnp.where((accept == 1)[:, None], replacement, first)
    return layer_call(n, second_in, stored_length, weights)


def solution(mesh):
    in_specs = (
        P(("req", "tp"), None),
        P(),
        P(),
        P(None, "tp"),
        P("tp"),
        P(),
        P(None, None, "tp"),
        P("tp", None),
        P(),
        P(),
        P(),
        P(None, "tp"),
        P("tp"),
        P("tp", None),
        P(),
        P("req", None, "tp"),
        P("req", None, "tp"),
        P("req"),
        P(),
        P(("req", "tp")),
        P("req"),
        P("req", "tp"),
    )
    out_specs = P(("req", "tp"), None)
    return jax.shard_map(shards, mesh=mesh, in_specs=in_specs, out_specs=out_specs, check_vma=False)
```

time: 433 us -> 290 us (0.67)
  waiting for transfers between devices: 297 us -> 37.1 us
  Pallas kernels: 0 us -> 205 us
  matrix products: 48.1 us -> 0 us
  local copies, waits for them, and re-layouts: 35 us -> 13.1 us
  other arithmetic: 22.4 us -> 3.52 us
    pallas_call x0 -> x2, Pallas kernels: none -> 205 us  [layer_call(): pl.pallas_call(functools.partial(layer_kernel, n, rows, heads), out_shape...]
    psum x4 -> x0, waiting for transfers between devices: 171 us -> none  [share_sum(): lax.psum(partial_sum.astype(jnp.bfloat16), 'tp').astype(jnp.float32)]
    all_gather x4 -> x0, waiting for transfers between devices: 79.8 us -> none  [the longest x2 49.8 us: run_layer_pass(): joined = project(lax.all_gather(normed, 'tp', axis=0, tiled=True))]
    dot_general x16 -> x0, matrix products: 48.1 us -> none  [the longest x4 18.6 us: share_sum(): partial_sum = jnp.dot(left, right, preferred_element_type=jnp.float32)]
    all_to_all x1, waiting for transfers between devices: 16.4 us -> 0.01 us  [shards(): lax.all_to_all(columns, 'tp', split_axis=0, concat_axis=1, tiled=True)]
    reduce_sum x13 -> x1, other arithmetic: 9 us -> 0.63 us  [shards(): tenant = jnp.sum((req_rank >= tenant_first_request).astype(jnp.int32))]
    convert_element_type x11 -> x1, other arithmetic: 10.6 us -> 2.71 us  [shards(): found = jnp.where(inside[:, None], found.astype(F32), 0.0).astype(BF16)]
    reduce_scatter x1, waiting for transfers between devices: 29.5 us -> 37.1 us  [shards(): columns = lax.psum_scatter(found, 'req', scatter_dimension=0, tiled=True)]
  transfers between devices with their start and end apart: 10 -> 2, of which waited for: 10 -> 1; matrix products, arithmetic and copies ran while one was open for 7% -> 1% of each run, Pallas kernels for 0% -> 39%
where the time goes in v1:
time: 290 us
  Pallas kernels  205 us (71%)
  waiting for transfers between devices  37.1 us (13%)
  between operations  16.3 us (6%)
  local copies, waits for them, and re-layouts  13.1 us (5%)
  blocking collectives  10.6 us (4%)
  starting transfers between devices  4.59 us (2%)
  other arithmetic  3.52 us (1%)
    pallas_call x2, Pallas kernels, layer_call(): pl.pallas_call(functools.partial(layer_kernel, n, rows, heads), out_shape...  205 us
    reduce_scatter x1, waiting for transfers between devices, shards(): columns = lax.psum_scatter(found, 'req', scatter_dimension=0, tiled=True)  37.1 us
    gather x1, local copies, waits for them, and re-layouts, shards(): jnp.take(word_embedding_table, jnp.clip(local_index, 0, table_rows - 1),...  11.2 us
    all_gather x1, blocking collectives, shards(): all_ids = lax.all_gather(replacement_token_index, 'req', axis=0, tiled=True)  10.6 us
  transfers between devices with their start and end apart: 2, of which 1 were waited for; matrix products, arithmetic and copies ran while one was open for 1% of the time, Pallas kernels for 39%

profile of v1, /device:TPU:0, one launch (start us, length us, event | category | flops | bytes accessed | tf_op | source)
XLA Modules:
  0.0 290.0 jit_solution(6317825295474567134)
XLA Ops:
  6.5 0.0 copy-start
  6.5 0.0 reduce-scatter.2.cloned.1.call-start
  6.5 10.6 %all-gather = s32[8,1,256]{2,1,0:T(1,128)S(1)} all-gather(s32[1,1,256]{2,1,0:T(1,128)} %bitcast.39), channel_id=1, replica_groups=mesh['req'=8,'tp'=4] {'req'}, dimensions={0}, use_global_device_ids=true | all-gather | bytes 9216 | tf_op jit(solution)/shard_map/all_gather | solution.py:393
  17.2 11.2 %gather_fusion = bf16[2048,512]{1,0:T(8,128)(2,1)S(1)} fusion(bf16[6272,512]{1,0:T(8,128)(2,1)} %param.43, s32[2048]{0:T(1024)S(1)} %fusion), kind=kCustom, calls=%fused_computation | custom fusion | bytes 4202496 | tf_op jit(solution)/shard_map/jit(_take)/gather | solution.py:396
  28.5 2.7 select_convert_fusion
  31.2 0.0 copy-start.3
  31.2 0.0 copy-start.4
  31.2 0.0 copy-start.5
  31.2 0.0 copy-start.6
  31.3 0.0 copy-start.7
  31.3 0.0 copy-start.8
  31.3 0.0 reduce-scatter.2.cloned.1.call-update
  32.1 0.0 copy-done.9
  32.1 0.0 copy-done.10
  32.1 0.6 fusion.1
  34.7 0.3 copy.28
  35.0 0.8 dynamic-slice_bitcast_fusion.au_ref
  35.8 37.1 %reduce-scatter.2.cloned.1.call-done = bf16[256,512]{1,0:T(8,128)(2,1)} async-done(((bf16[2048,512]{1,0:T(8,128)(2,1)}), bf16[256,512]{1,0:T(8,128)(2,1)}) %reduce-scatter.2.cloned.1.call-update) | async-done | bytes 262160 | tf_op jit(solution)/shard_map/reduce_scatter | solution.py:398
  72.9 4.6 %all-to-all-start = ((bf16[4,64,512]{2,1,0:T(8,128)(2,1)}), bf16[4,64,512]{2,1,0:T(8,128)(2,1)S(1)}, u32[]{:S(2)}, u32[]{:S(2)}) async-start(bf16[4,64,512]{2,1,0:T(8,128)(2,1)} %bitcast.36), calls=%async_computation.1 | async-start | bytes 524288 | tf_op jit(solution)/shard_map/all_to_all | solution.py:399
  77.5 0.0 copy-done.3
  77.5 0.0 copy-done.4
  77.5 0.0 copy-done.5
  77.5 0.0 copy-done.6
  77.5 0.0 copy-done.7
  77.5 0.0 copy-done.8
  77.5 0.0 copy-start.11
  77.5 112.3 %layer_pass.2 = bf16[64,2048]{1,0:T(8,128)(2,1)S(1)} custom-call(s32[1]{0:T(128)S(6)} %copy.31.length_ref, bf16[64,2048]{1,0:T(8,128)(2,1)S(1)} %copy-done.1, f32[1,2048]{1,0:T(1,128)S(1)} %bitcast.20, f32[1,2048]{1,0:T(1,128)S(1)} %bitcast.22, bf16[2048,1536]{1,0:T(8,128)(2,1)} %wq_hbm.3, f32[1,1536]{1,0:T(1,128)S(1)} %broadcast_in_dim.66.bq_ref, ...), custom_call_target="tpu_custom_call" | custom-call | flops 8999999488 | bytes 20000000 | tf_op jit(solution)/shard_map/layer_pass/pallas_call | solution.py:321
  189.9 0.0 copy-done.11
  189.9 0.0 all-to-all-done
  189.9 0.1 broadcast_select_fusion.x_ref
  190.0 92.5 %layer_pass.3 = bf16[64,2048]{1,0:T(8,128)(2,1)S(1)} custom-call(s32[1]{0:T(128)S(6)} %copy.31.length_ref, bf16[64,2048]{1,0:T(8,128)(2,1)S(1)} %broadcast_select_fusion.x_ref, f32[1,2048]{1,0:T(1,128)S(1)} %bitcast.21, f32[1,2048]{1,0:T(1,128)S(1)} %bitcast.23, bf16[2048,1536]{1,0:T(8,128)(2,1)} %wq_hbm.3, f32[1,1536]{1,0:T(1,128)S(1)} %broadcast_in_dim.66.bq_ref, ...), custom_call_target="tpu_custom_call" | custom-call | flops 8999999488 | bytes 20000000 | tf_op jit(solution)/shard_map/layer_pass/pallas_call | solution.py:321
  282.5 0.7 copy.32
  (16 shorter events, 0.1 us)
Async XLA Ops:
  6.5 28.1 %copy-start = (bf16[4,2048,16]{1,2,0:T(8,128)(2,1)S(1)}, bf16[4,2048,16]{1,2,0:T(8,128)(2,1)}, u32[]{:S(2)}) copy-start(bf16[4,2048,16]{1,2,0:T(8,128)(2,1)} %param.27) | copy-start | bytes 786436
  6.5 66.3 %reduce-scatter.2.cloned.1.call-start = ((), (), s32[]{:S(2)}) async-start(), calls=%async_computation.2 | async-start | bytes 2359296 | tf_op jit(solution)/shard_map/reduce_scatter | solution.py:398
  31.2 0.9 copy-start.9
  31.2 0.9 copy-start.10
  31.2 46.3 %copy-start.1 = (bf16[64,2048]{1,0:T(8,128)(2,1)S(1)}, bf16[64,2048]{1,0:T(8,128)(2,1)}, u32[]{:S(2)}) copy-start(bf16[64,2048]{1,0:T(8,128)(2,1)} %x_ref.1) | copy-start | bytes 786436
  31.2 46.3 %copy-start.2 = (f32[2048]{0:T(1024)S(1)}, f32[2048]{0:T(1024)}, u32[]{:S(2)}) copy-start(f32[2048]{0:T(1024)} %param.23) | copy-start | bytes 24580
  31.2 46.3 %copy-start.3 = (f32[2048]{0:T(1024)S(1)}, f32[2048]{0:T(1024)}, u32[]{:S(2)}) copy-start(f32[2048]{0:T(1024)} %param.24) | copy-start | bytes 24580
  31.2 46.2 %copy-start.4 = (f32[2048]{0:T(1024)S(1)}, f32[2048]{0:T(1024)}, u32[]{:S(2)}) copy-start(f32[2048]{0:T(1024)} %param.30) | copy-start | bytes 24580
  31.2 46.2 %copy-start.5 = (f32[2048]{0:T(1024)S(1)}, f32[2048]{0:T(1024)}, u32[]{:S(2)}) copy-start(f32[2048]{0:T(1024)} %param.31) | copy-start | bytes 24580
  31.2 46.2 %copy-start.6 = (f32[2048]{0:T(1024)S(1)}, f32[2048]{0:T(1024)}, u32[]{:S(2)}) copy-start(f32[2048]{0:T(1024)} %param.32) | copy-start | bytes 24580
  31.3 46.2 %copy-start.7 = (f32[2048]{0:T(1024)S(1)}, f32[2048]{0:T(1024)}, u32[]{:S(2)}) copy-start(f32[2048]{0:T(1024)} %param.36) | copy-start | bytes 24580
  31.3 46.2 %copy-start.8 = (f32[1024]{0:T(1024)S(1)}, f32[1024]{0:T(1024)}, u32[]{:S(2)}) copy-start(f32[1024]{0:T(1024)} %param.34) | copy-start | bytes 12292
  72.9 117.0 %all-to-all-start = ((bf16[4,64,512]{2,1,0:T(8,128)(2,1)}), bf16[4,64,512]{2,1,0:T(8,128)(2,1)S(1)}, u32[]{:S(2)}, u32[]{:S(2)}) async-start(bf16[4,64,512]{2,1,0:T(8,128)(2,1)} %bitcast.36), calls=%async_computation.1 | async-start | bytes 524288 | tf_op jit(solution)/shard_map/all_to_all | solution.py:399
  77.5 112.4 %copy-start.11 = (s32[64]{0:T(128)S(1)}, s32[64]{0:T(128)}, u32[]{:S(2)}) copy-start(s32[64]{0:T(128)} %param.41) | copy-start | bytes 772
Sparse Core Ops, SparseCore 0:
  31.4 41.3 reduce-scatter.1

commit v2 on v1

v2 whole, which is shorter than its diff:
```python
import functools

import jax
import jax.numpy as jnp
from jax import lax
from jax.experimental import pallas as pl
from jax.experimental.pallas import tpu as pltpu
from jax.sharding import PartitionSpec as P

H = 16
HD = 128
BLK = 256
EPSILON = 1e-05
F32 = jnp.float32
BF16 = jnp.bfloat16


def norm_rows(values, gain, shift):
    mean = jnp.mean(values, axis=-1, keepdims=True)
    centered = values - mean
    variance = jnp.mean(centered * centered, axis=-1, keepdims=True)
    return (centered * lax.rsqrt(variance + EPSILON) * gain + shift).astype(BF16)


def layer_kernel(n, n_req, rows, heads, embed, *refs):
    refs = iter(refs)
    take = lambda count: [next(refs) for _ in range(count)]
    length_ref, x_ref, in_gain, in_shift, wq_hbm, bq_ref, ad_ref, au_ref = take(8)
    wo_hbm, bo_ref, post_gain, post_shift, wu_hbm, bu_ref, wd_hbm, bd_ref, kc_hbm, vc_hbm = take(10)
    if embed:
        found_ref, pick_ref, accept_ref = take(3)
    (out_ref,) = take(1)
    wq, wo, wu, wd, kc, vc = take(6)
    states, normed, post, attended, part_a, part_b = take(6)
    from_left_a, from_right_a, to_left, to_right, from_left_b, from_right_b = take(6)
    qkv, ctx, hid = take(3)
    load_sem, gat_send_right, gat_send_left, gat_recv = take(4)
    line_send_right, line_send_left, line_recv_left, line_recv_right = take(4)
    sum_send, sum_recv_left, sum_recv_right = take(3)
    if embed:
        landed, picked, replaced, row_send, row_recv, col_send, col_recv = take(7)
    mesh_id = pl.DeviceIdType.MESH
    me = lax.axis_index("tp")
    mine = lax.axis_index("req")
    loads = [
        pltpu.make_async_copy(source, target, load_sem.at[index])
        for index, (source, target) in enumerate(
            ((wq_hbm, wq), (kc_hbm, kc), (vc_hbm, vc), (wo_hbm, wo), (wu_hbm, wu), (wd_hbm, wd))
        )
    ]
    for load in loads:
        load.start()
    has_left = me > 0
    has_right = me < n - 1

    barrier = pltpu.get_barrier_semaphore()
    if embed:
        for k in range(1, n):
            pl.semaphore_signal(
                barrier, inc=1, device_id={"tp": lax.rem(me + k, n)}, device_id_type=mesh_id
            )
        for k in range(1, n_req):
            pl.semaphore_signal(
                barrier, inc=1, device_id={"req": lax.rem(mine + k, n_req)}, device_id_type=mesh_id
            )
    else:

        @pl.when(has_left)
        def _():
            pl.semaphore_signal(barrier, inc=1, device_id={"tp": me - 1}, device_id_type=mesh_id)

        @pl.when(has_right)
        def _():
            pl.semaphore_signal(barrier, inc=1, device_id={"tp": me + 1}, device_id_type=mesh_id)

    def chunk(index):
        return pl.ds(pl.multiple_of(index * rows, rows), rows)

    def zero(buffer):
        buffer[...] = jnp.zeros(buffer.shape, buffer.dtype)

    states[chunk(me), :] = x_ref[...]

    @pl.when(jnp.logical_not(has_left))
    def _():
        zero(from_left_a)

    @pl.when(jnp.logical_not(has_right))
    def _():
        zero(from_right_a)

    if embed:
        pl.semaphore_wait(barrier, n - 1 + n_req - 1)
    else:
        pl.semaphore_wait(barrier, has_left.astype(jnp.int32) + has_right.astype(jnp.int32))

    def gather_copy(index, step):
        sends = gat_send_right if step > 0 else gat_send_left
        return pltpu.make_async_remote_copy(
            src_ref=states.at[chunk(index), :],
            dst_ref=states.at[chunk(index), :],
            send_sem=sends.at[index],
            recv_sem=gat_recv.at[index],
            device_id={"tp": me + step},
            device_id_type=mesh_id,
        )

    def norm_in(index):
        normed[chunk(index), :] = norm_rows(
            states[chunk(index), :].astype(F32), in_gain[...], in_shift[...]
        )

    @pl.when(has_right)
    def _():
        gather_copy(me, 1).start()

    @pl.when(has_left)
    def _():
        gather_copy(me, -1).start()

    if embed:
        cap = found_ref.shape[0] // n_req

        def row_block(index):
            return pl.ds(pl.multiple_of(index * cap, cap), cap)

        def row_copy(peer, source):
            return pltpu.make_async_remote_copy(
                src_ref=found_ref.at[row_block(peer), :],
                dst_ref=landed.at[row_block(source), :],
                send_sem=row_send.at[peer],
                recv_sem=row_recv.at[source],
                device_id={"req": peer},
                device_id_type=mesh_id,
            )

        for k in range(1, n_req):
            row_copy(lax.rem(mine + k, n_req), mine).start()
        landed[row_block(mine), :] = found_ref[row_block(mine), :]

    norm_in(me)
    for k in range(1, n):

        @pl.when(me - k >= 0)
        def _():
            gather_copy(me - k, 1).wait_recv()

            @pl.when(has_right)
            def _():
                gather_copy(me - k, 1).start()

        @pl.when(me + k <= n - 1)
        def _():
            gather_copy(me + k, -1).wait_recv()

            @pl.when(has_left)
            def _():
                gather_copy(me + k, -1).start()

        @pl.when(me - k >= 0)
        def _():
            norm_in(me - k)

        @pl.when(me + k <= n - 1)
        def _():
            norm_in(me + k)

    def columns(index, width):
        return pl.ds(pl.multiple_of(index * width, width), width)

    loads[0].wait()
    low = jnp.dot(normed[...], ad_ref[...], preferred_element_type=F32).astype(BF16)

    @pl.loop(0, wq.shape[1] // 256)
    def _(tile):
        cols = columns(tile, 256)
        joined = jnp.dot(normed[...], wq[:, cols], preferred_element_type=F32)
        joined = joined + jnp.dot(low, au_ref[:, cols], preferred_element_type=F32)
        qkv[:, cols] = (joined + bq_ref[:, cols]).astype(BF16)

    if embed:
        for k in range(1, n_req):
            peer = lax.rem(mine + k, n_req)
            row_copy(peer, peer).wait_recv()
        slots = lax.broadcasted_iota(jnp.int32, (pick_ref.shape[0], landed.shape[0]), 1)
        chosen = jnp.where(slots == pick_ref[...], 1.0, 0.0).astype(BF16)
        picked[...] = jnp.dot(chosen, landed[...], preferred_element_type=F32).astype(BF16)

        def column_copy(peer, source):
            return pltpu.make_async_remote_copy(
                src_ref=picked.at[chunk(peer), :],
                dst_ref=replaced.at[source],
                send_sem=col_send.at[peer],
                recv_sem=col_recv.at[source],
                device_id={"tp": peer},
                device_id_type=mesh_id,
            )

        for k in range(1, n):
            column_copy(lax.rem(me + k, n), me).start()
        replaced[me] = picked[chunk(me), :]

    loads[1].wait()
    loads[2].wait()
    length = length_ref[0]
    cache_rows = kc.shape[0]
    block = qkv.shape[0]
    scale = HD**-0.5

    @pl.loop(0, heads)
    def _(head):
        exponent = jnp.zeros((1, 1), F32) + (me * heads + head + 1).astype(F32) * (-8.0 / H)
        slope = jnp.exp2(exponent)
        query = qkv[:, columns(head * 3, HD)]
        key = qkv[:, columns(head * 3 + 1, HD)]
        value = qkv[:, columns(head * 3 + 2, HD)]
        contract = (((1,), (1,)), ((), ()))
        block_scores = lax.dot_general(query, key, contract, preferred_element_type=F32) * scale
        q_pos = lax.broadcasted_iota(jnp.int32, (block, 1), 0)
        k_pos = lax.broadcasted_iota(jnp.int32, (1, block), 1)
        block_scores = block_scores - slope * jnp.abs(q_pos - k_pos).astype(F32)
        cache_scores = (
            lax.dot_general(query, kc[:, columns(head, HD)], contract, preferred_element_type=F32)
            * scale
        )
        c_pos = lax.broadcasted_iota(jnp.int32, (1, cache_rows), 1)
        cache_scores = cache_scores - slope * (q_pos + length - c_pos).astype(F32)
        cache_scores = jnp.where(c_pos < length, cache_scores, -jnp.inf)
        top = jnp.maximum(
            jnp.max(block_scores, axis=-1, keepdims=True),
            jnp.max(cache_scores, axis=-1, keepdims=True),
        )
        block_weights = jnp.exp(block_scores - top)
        cache_weights = jnp.exp(cache_scores - top)
        total = jnp.sum(block_weights, axis=-1, keepdims=True) + jnp.sum(
            cache_weights, axis=-1, keepdims=True
        )
        mixed = jnp.dot(block_weights.astype(BF16), value, preferred_element_type=F32)
        mixed = mixed + jnp.dot(
            cache_weights.astype(BF16), vc[:, columns(head, HD)], preferred_element_type=F32
        )
        ctx[:, columns(head, HD)] = (mixed / total).astype(BF16)

    loads[3].wait()

    @pl.loop(0, wo.shape[1] // 256)
    def _(tile):
        cols = columns(tile, 256)
        part_a[:, cols] = jnp.dot(ctx[...], wo[:, cols], preferred_element_type=F32).astype(BF16)

    piece_rows = 16
    pieces = block // piece_rows

    def piece(index):
        return pl.ds(pl.multiple_of(index * piece_rows, piece_rows), piece_rows)

    def line_right(index):
        return pltpu.make_async_remote_copy(
            src_ref=to_right.at[piece(index), :],
            dst_ref=from_left_a.at[piece(index), :],
            send_sem=line_send_right.at[index],
            recv_sem=line_recv_left.at[index],
            device_id={"tp": me + 1},
            device_id_type=mesh_id,
        )

    def line_left(index):
        return pltpu.make_async_remote_copy(
            src_ref=to_left.at[piece(index), :],
            dst_ref=from_right_a.at[piece(index), :],
            send_sem=line_send_left.at[index],
            recv_sem=line_recv_right.at[index],
            device_id={"tp": me - 1},
            device_id_type=mesh_id,
        )

    @pl.loop(0, pieces + n - 1)
    def _(step):
        right_piece = step - me
        left_piece = step - (n - 1 - me)
        done_piece = step - (n - 1)

        @pl.when((right_piece >= 0) & (right_piece < pieces))
        def _():
            @pl.when(has_left)
            def _():
                line_right(right_piece).wait_recv()

            @pl.when(has_right)
            def _():
                here = piece(right_piece)
                to_right[here, :] = (
                    part_a[here, :].astype(F32) + from_left_a[here, :].astype(F32)
                ).astype(BF16)
                line_right(right_piece).start()

        @pl.when((left_piece >= 0) & (left_piece < pieces))
        def _():
            @pl.when(has_right)
            def _():
                line_left(left_piece).wait_recv()

            @pl.when(has_left)
            def _():
                here = piece(left_piece)
                to_left[here, :] = (
                    part_a[here, :].astype(F32) + from_right_a[here, :].astype(F32)
                ).astype(BF16)
                line_left(left_piece).start()

        @pl.when(done_piece >= 0)
        def _():
            here = piece(done_piece)
            summed = part_a[here, :].astype(F32) + from_left_a[here, :].astype(F32)
            summed = summed + from_right_a[here, :].astype(F32)
            summed = (states[here, :].astype(F32) + summed + bo_ref[...]).astype(BF16)
            attended[here, :] = summed
            post[here, :] = norm_rows(summed.astype(F32), post_gain[...], post_shift[...])

    loads[4].wait()

    @pl.loop(0, wu.shape[1] // 256)
    def _(tile):
        cols = columns(tile, 256)
        inner = jnp.dot(post[...], wu[:, cols], preferred_element_type=F32) + bu_ref[:, cols]
        hid[:, cols] = jax.nn.gelu(inner, approximate=True).astype(BF16)

    loads[5].wait()

    @pl.loop(0, wd.shape[1] // 256)
    def _(tile):
        cols = columns(tile, 256)
        part_b[:, cols] = jnp.dot(hid[...], wd[:, cols], preferred_element_type=F32).astype(BF16)

    def sum_copy(landing, index, step):
        recvs = sum_recv_left if step > 0 else sum_recv_right
        return pltpu.make_async_remote_copy(
            src_ref=part_b.at[chunk(index), :],
            dst_ref=landing.at[chunk(index), :],
            send_sem=sum_send.at[index],
            recv_sem=recvs.at[index],
            device_id={"tp": me + step},
            device_id_type=mesh_id,
        )

    def add_in(landing, index):
        part_b[chunk(index), :] = (
            part_b[chunk(index), :].astype(F32) + landing[chunk(index), :].astype(F32)
        ).astype(BF16)

    for k in range(n - 1):
        right_index = n - 1 - k
        left_index = k

        @pl.when(right_index > me)
        def _():
            @pl.when(has_left)
            def _():
                sum_copy(from_left_b, right_index, 1).wait_recv()
                add_in(from_left_b, right_index)

            sum_copy(from_left_b, right_index, 1).start()

        @pl.when(left_index < me)
        def _():
            @pl.when(has_right)
            def _():
                sum_copy(from_right_b, left_index, -1).wait_recv()
                add_in(from_right_b, left_index)

            sum_copy(from_right_b, left_index, -1).start()

    @pl.when(has_left)
    def _():
        sum_copy(from_left_b, me, 1).wait_recv()
        add_in(from_left_b, me)

    @pl.when(has_right)
    def _():
        sum_copy(from_right_b, me, -1).wait_recv()
        add_in(from_right_b, me)

    result = (
        attended[chunk(me), :].astype(F32) + part_b[chunk(me), :].astype(F32) + bd_ref[...]
    ).astype(BF16)
    if embed:
        width = replaced.shape[2]
        for k in range(1, n):
            peer = lax.rem(me + k, n)
            column_copy(peer, peer).wait_recv()
        for k in range(n):
            cols = slice(k * width, (k + 1) * width)
            out_ref[:, cols] = jnp.where(accept_ref[...] == 1, replaced[k], result[:, cols])
        for k in range(1, n):
            column_copy(lax.rem(me + k, n), me).wait_send()
        for k in range(1, n_req):
            row_copy(lax.rem(mine + k, n_req), mine).wait_send()
    else:
        out_ref[...] = result

    for k in range(n):

        @pl.when((me - k >= 0) & has_right)
        def _():
            gather_copy(me - k, 1).wait_send()

        @pl.when((me + k <= n - 1) & has_left)
        def _():
            gather_copy(me + k, -1).wait_send()

        @pl.when(k > me)
        def _():
            sum_copy(from_left_b, k, 1).wait_send()

        @pl.when(k < me)
        def _():
            sum_copy(from_right_b, k, -1).wait_send()

    @pl.loop(0, pieces)
    def _(index):
        @pl.when(has_right)
        def _():
            line_right(index).wait_send()

        @pl.when(has_left)
        def _():
            line_left(index).wait_send()


def layer_call(n, n_req, x, length, weights, extra):
    rows, width = x.shape
    wq, wo, wu, wd, kc, vc = weights[2], weights[6], weights[10], weights[12], weights[14], weights[15]
    heads = wo.shape[0] // HD
    block = n * rows
    embed = len(extra) > 0
    vmem = pl.BlockSpec(memory_space=pltpu.VMEM)
    hbm = pl.BlockSpec(memory_space=pl.ANY)
    smem = pl.BlockSpec(memory_space=pltpu.SMEM)
    in_hbm = (2, 6, 10, 12, 14, 15)
    specs = [smem, vmem] + [hbm if i in in_hbm else vmem for i in range(len(weights))]
    specs = specs + [vmem] * len(extra)
    full = pltpu.VMEM((block, width), BF16)
    dma = pltpu.SemaphoreType.DMA
    scratch = [pltpu.VMEM(a.shape, BF16) for a in (wq, wo, wu, wd, kc, vc)] + [full] * 12
    scratch = scratch + [
        pltpu.VMEM((block, wq.shape[1]), BF16),
        pltpu.VMEM((block, wo.shape[0]), BF16),
        pltpu.VMEM((block, wu.shape[1]), BF16),
        dma((6,)),
    ]
    scratch = scratch + [dma((n,))] * 3 + [dma((block // 16,))] * 4 + [dma((n,))] * 3
    if embed:
        part = extra[0].shape[1]
        scratch = scratch + [
            pltpu.VMEM(extra[0].shape, BF16),
            pltpu.VMEM((block, part), BF16),
            pltpu.VMEM((n, rows, part), BF16),
            dma((n_req,)),
            dma((n_req,)),
            dma((n,)),
            dma((n,)),
        ]
    return pl.pallas_call(
        functools.partial(layer_kernel, n, n_req, rows, heads, embed),
        out_shape=jax.ShapeDtypeStruct((rows, width), BF16),
        in_specs=specs,
        out_specs=vmem,
        scratch_shapes=scratch,
        compiler_params=pltpu.CompilerParams(
            collective_id=1 if embed else 0,
            has_side_effects=True,
            vmem_limit_bytes=54 * 2**20,
        ),
        cost_estimate=pl.CostEstimate(
            flops=9_000_000_000, bytes_accessed=20_000_000, transcendentals=1_500_000
        ),
        name="first_pass" if embed else "second_pass",
    )(length, x, *weights, *extra)


def shards(
    embeds,
    input_norm_gain,
    input_norm_bias,
    joined_projection_weight,
    joined_projection_bias,
    adapter_down_weight,
    adapter_up_weight,
    attention_out_weight,
    attention_out_bias,
    post_attention_norm_gain,
    post_attention_norm_bias,
    feedforward_up_weight,
    feedforward_up_bias,
    feedforward_down_weight,
    feedforward_down_bias,
    stored_keys,
    stored_values,
    stored_length,
    tenant_first_request,
    accept,
    replacement_token_index,
    word_embedding_table,
):
    n = lax.axis_size("tp")
    req_rank = lax.axis_index("req")
    table_rows = word_embedding_table.shape[0]
    tenant = jnp.sum((req_rank >= tenant_first_request).astype(jnp.int32))
    weights = (
        input_norm_gain[None],
        input_norm_bias[None],
        joined_projection_weight,
        joined_projection_bias[None],
        lax.dynamic_index_in_dim(adapter_down_weight, tenant, 0, keepdims=False),
        lax.dynamic_index_in_dim(adapter_up_weight, tenant, 0, keepdims=False),
        attention_out_weight,
        attention_out_bias[None],
        post_attention_norm_gain[None],
        post_attention_norm_bias[None],
        feedforward_up_weight,
        feedforward_up_bias[None],
        feedforward_down_weight,
        feedforward_down_bias[None],
        stored_keys[0],
        stored_values[0],
    )

    n_req = lax.axis_size("req")
    block = replacement_token_index.shape[0]
    cap = (3 * block // n_req + 15) // 16 * 16
    owner = replacement_token_index // table_rows
    place = jnp.arange(block)
    earlier = (owner[:, None] == owner[None, :]) & (place[None, :] < place[:, None])
    rank = jnp.sum(earlier.astype(jnp.int32), axis=1)
    pick = (owner * cap + rank)[:, None]

    all_ids = lax.all_gather(replacement_token_index, "req", axis=0)
    local_index = all_ids - req_rank * table_rows
    inside = (local_index >= 0) & (local_index < table_rows)
    before = (place[:, None] < place[None, :]).astype(BF16)
    slot = jnp.dot(inside.astype(BF16), before, preferred_element_type=F32).astype(jnp.int32)
    slot = jnp.where(inside, slot, -1)
    hit = slot[:, None, :] == jnp.arange(cap)[None, :, None]
    wanted = jnp.sum(jnp.where(hit, local_index[:, None, :], 0), axis=2).reshape(-1)
    found = word_embedding_table.at[wanted].get(mode="promise_in_bounds")
    extra = (found, pick, accept[:, None])
    second_in = layer_call(n, n_req, embeds, stored_length, weights, extra)
    return layer_call(n, n_req, second_in, stored_length, weights, ())


def solution(mesh):
    in_specs = (
        P(("req", "tp"), None),
        P(),
        P(),
        P(None, "tp"),
        P("tp"),
        P(),
        P(None, None, "tp"),
        P("tp", None),
        P(),
        P(),
        P(),
        P(None, "tp"),
        P("tp"),
        P("tp", None),
        P(),
        P("req", None, "tp"),
        P("req", None, "tp"),
        P("req"),
        P(),
        P(("req", "tp")),
        P("req"),
        P("req", "tp"),
    )
    out_specs = P(("req", "tp"), None)
    return jax.shard_map(shards, mesh=mesh, in_specs=in_specs, out_specs=out_specs, check_vma=False)
```

time: 290 us -> 274 us (0.945)
  Pallas kernels: 205 us -> 243 us
  waiting for transfers between devices: 37.1 us -> 0 us
  between operations: 16.3 us -> 2.69 us
  starting transfers between devices: 4.59 us -> 0 us
    pallas_call x2, Pallas kernels: 205 us -> 243 us  [layer_call(): pl.pallas_call(functools.partial(layer_kernel, n, n_req, rows, heads, emb...]
    reduce_scatter x1 -> x0, waiting for transfers between devices: 37.1 us -> none  [shards(): columns = lax.psum_scatter(found, 'req', scatter_dimension=0, tiled=True)]
    all_to_all x1 -> x0, starting transfers between devices: 4.59 us -> none  [shards(): lax.all_to_all(columns, 'tp', split_axis=0, concat_axis=1, tiled=True)]
    gather x1, local copies, waits for them, and re-layouts: 11.2 us -> 7.01 us  [shards(): found = word_embedding_table.at[wanted].get(mode='promise_in_bounds')]
  transfers between devices with their start and end apart: 2 -> 0, of which waited for: 1 -> 0; matrix products, arithmetic and copies ran while one was open for 1% -> 0% of each run, Pallas kernels for 39% -> 0%
where the time goes in v2:
time: 274 us
  Pallas kernels  243 us (89%)
  local copies, waits for them, and re-layouts  14.6 us (5%)
  blocking collectives  10.5 us (4%)
  other arithmetic  3.11 us (1%)
    pallas_call x2, Pallas kernels, layer_call(): pl.pallas_call(functools.partial(layer_kernel, n, n_req, rows, heads, emb...  243 us
    all_gather x1, blocking collectives, shards(): all_ids = lax.all_gather(replacement_token_index, 'req', axis=0)  10.5 us
    gather x1, local copies, waits for them, and re-layouts, shards(): found = word_embedding_table.at[wanted].get(mode='promise_in_bounds')  7.01 us

profile of v2, /device:TPU:0, one launch (start us, length us, event | category | flops | bytes accessed | tf_op | source)
XLA Modules:
  0.0 274.0 jit_solution(16911398085828256448)
XLA Ops:
  0.0 0.0 copy-start
  0.7 1.3 fusion.9
  3.9 0.7 and_select_fusion
  4.6 0.2 convert_reduce_fusion
  4.8 0.7 multiply_add_fusion
  5.5 1.3 broadcast_in_dim.58.refs_5_
  6.8 10.5 %all-gather.1 = s32[8,1,256]{2,1,0:T(1,128)S(1)} all-gather(s32[1,1,256]{2,1,0:T(1,128)} %bitcast.19), channel_id=2, replica_groups=mesh['req'=8,'tp'=4] {'req'}, dimensions={0}, use_global_device_ids=true | all-gather | bytes 9216 | tf_op jit(solution)/shard_map/all_gather | solution.py:537
  17.3 0.2 fusion
  17.4 0.2 select_reduce_fusion
  17.7 0.1 reshape.35
  17.8 1.3 copy.35.refs_20_
  19.1 1.4 dynamic-slice_bitcast_fusion.refs_7_
  20.5 0.0 copy-done
  20.5 0.8 copy.34.refs_19_
  21.3 1.0 copy.32
  22.4 7.0 %gather_fusion = bf16[768,512]{1,0:T(8,128)(2,1)} fusion(bf16[6272,512]{1,0:T(8,128)(2,1)} %param.43, s32[1024]{0:T(1024)S(1)} %pad_clamp_fusion), kind=kCustom, calls=%fused_computation | custom fusion | bytes 1575936 | tf_op jit(solution)/shard_map/gather | solution.py:545
  29.4 130.5 %first_pass.1.refs_1_ = bf16[64,2048]{1,0:T(8,128)(2,1)} custom-call(s32[1]{0:T(128)S(6)} %copy.40.refs_0_, bf16[64,2048]{1,0:T(8,128)(2,1)} %refs_1_.1, f32[1,2048]{1,0:T(1,128)} %bitcast.26, f32[1,2048]{1,0:T(1,128)} %bitcast.28, bf16[2048,1536]{1,0:T(8,128)(2,1)} %refs_4_.3, f32[1,1536]{1,0:T(1,128)} %broadcast_in_dim.58.refs_5_, ...), custom_call_target="tpu_custom_call" | custom-call | flops 8999999488 | bytes 20000000 | tf_op jit(solution)/shard_map/first_pass/pallas_call | solution.py:463
  159.9 112.4 %second_pass.1 = bf16[64,2048]{1,0:T(8,128)(2,1)} custom-call(s32[1]{0:T(128)S(6)} %copy.40.refs_0_, bf16[64,2048]{1,0:T(8,128)(2,1)} %first_pass.1.refs_1_, f32[1,2048]{1,0:T(1,128)} %bitcast.27, f32[1,2048]{1,0:T(1,128)} %bitcast.29, bf16[2048,1536]{1,0:T(8,128)(2,1)} %refs_4_.3, f32[1,1536]{1,0:T(1,128)} %broadcast_in_dim.58.refs_5_, ...), custom_call_target="tpu_custom_call" | custom-call | flops 8999999488 | bytes 20000000 | tf_op jit(solution)/shard_map/second_pass/pallas_call | solution.py:463
  272.3 1.7 copy.41
  (4 shorter events, 0.0 us)
Async XLA Ops:
  0.0 20.5 %copy-start = (bf16[4,2048,16]{1,2,0:T(8,128)(2,1)S(1)}, bf16[4,2048,16]{1,2,0:T(8,128)(2,1)}, u32[]{:S(2)}) copy-start(bf16[4,2048,16]{1,2,0:T(8,128)(2,1)} %param.27) | copy-start | bytes 786436

commit v3 on v2

--- a/solution.py
+++ b/solution.py
@@ -249,6 +249,7 @@
         part_a[:, cols] = jnp.dot(ctx[...], wo[:, cols], preferred_element_type=F32).astype(BF16)
 
     piece_rows = 16
+    lag = 5
     pieces = block // piece_rows
 
     def piece(index):
@@ -274,11 +275,11 @@
             device_id_type=mesh_id,
         )
 
-    @pl.loop(0, pieces + n - 1)
+    @pl.loop(0, pieces + lag * (n - 1))
     def _(step):
-        right_piece = step - me
-        left_piece = step - (n - 1 - me)
-        done_piece = step - (n - 1)
+        right_piece = step - lag * me
+        left_piece = step - lag * (n - 1 - me)
+        done_piece = step - lag * (n - 1)
 
         @pl.when((right_piece >= 0) & (right_piece < pieces))
         def _():
@@ -528,7 +529,7 @@
     n_req = lax.axis_size("req")
     block = replacement_token_index.shape[0]
     cap = (3 * block // n_req + 15) // 16 * 16
-    owner = replacement_token_index // table_rows
+    owner = lax.div(replacement_token_index, jnp.int32(table_rows))
     place = jnp.arange(block)
     earlier = (owner[:, None] == owner[None, :]) & (place[None, :] < place[:, None])
     rank = jnp.sum(earlier.astype(jnp.int32), axis=1)

time: 274 us -> 213 us (0.78)
  Pallas kernels: 243 us -> 182 us
    pallas_call x2, Pallas kernels: 243 us -> 182 us  [layer_call(): pl.pallas_call(functools.partial(layer_kernel, n, n_req, rows, heads, emb...]
where the time goes in v3:
time: 213 us
  Pallas kernels  182 us (85%)
  local copies, waits for them, and re-layouts  14.6 us (7%)
  blocking collectives  10.5 us (5%)
  other arithmetic  3.11 us (1%)
  between operations  2.69 us (1%)
    pallas_call x2, Pallas kernels, layer_call(): pl.pallas_call(functools.partial(layer_kernel, n, n_req, rows, heads, emb...  182 us
    all_gather x1, blocking collectives, shards(): all_ids = lax.all_gather(replacement_token_index, 'req', axis=0)  10.5 us
    gather x1, local copies, waits for them, and re-layouts, shards(): found = word_embedding_table.at[wanted].get(mode='promise_in_bounds')  7.01 us

profile of v3, /device:TPU:0, one launch (start us, length us, event | category | flops | bytes accessed | tf_op | source)
XLA Modules:
  0.0 212.9 jit_solution(2847986842363827466)
XLA Ops:
  0.0 0.0 copy-start
  0.7 1.3 fusion.9
  3.9 0.7 broadcast_divide_fusion
  4.6 0.2 convert_reduce_fusion
  4.8 0.7 multiply_add_fusion
  5.5 1.3 broadcast_in_dim.58.refs_5_
  6.8 10.5 %all-gather.1 = s32[8,1,256]{2,1,0:T(1,128)S(1)} all-gather(s32[1,1,256]{2,1,0:T(1,128)} %bitcast.19), channel_id=2, replica_groups=mesh['req'=8,'tp'=4] {'req'}, dimensions={0}, use_global_device_ids=true | all-gather | bytes 9216 | tf_op jit(solution)/shard_map/all_gather | solution.py:538
  17.3 0.2 fusion
  17.4 0.2 select_reduce_fusion
  17.6 0.1 reshape.35
  17.8 1.3 copy.35.refs_20_
  19.1 1.4 dynamic-slice_bitcast_fusion.refs_7_
  20.5 0.0 copy-done
  20.5 0.8 copy.34.refs_19_
  21.3 1.0 copy.32
  22.3 7.0 %gather_fusion = bf16[768,512]{1,0:T(8,128)(2,1)} fusion(bf16[6272,512]{1,0:T(8,128)(2,1)} %param.43, s32[1024]{0:T(1024)S(1)} %pad_clamp_fusion), kind=kCustom, calls=%fused_computation | custom fusion | bytes 1575936 | tf_op jit(solution)/shard_map/gather | solution.py:546
  29.3 104.8 %first_pass.1.refs_1_ = bf16[64,2048]{1,0:T(8,128)(2,1)} custom-call(s32[1]{0:T(128)S(6)} %copy.40.refs_0_, bf16[64,2048]{1,0:T(8,128)(2,1)} %refs_1_.1, f32[1,2048]{1,0:T(1,128)} %bitcast.26, f32[1,2048]{1,0:T(1,128)} %bitcast.28, bf16[2048,1536]{1,0:T(8,128)(2,1)} %refs_4_.3, f32[1,1536]{1,0:T(1,128)} %broadcast_in_dim.58.refs_5_, ...), custom_call_target="tpu_custom_call" | custom-call | flops 8999999488 | bytes 20000000 | tf_op jit(solution)/shard_map/first_pass/pallas_call | solution.py:464
  134.2 77.1 %second_pass.1 = bf16[64,2048]{1,0:T(8,128)(2,1)} custom-call(s32[1]{0:T(128)S(6)} %copy.40.refs_0_, bf16[64,2048]{1,0:T(8,128)(2,1)} %first_pass.1.refs_1_, f32[1,2048]{1,0:T(1,128)} %bitcast.27, f32[1,2048]{1,0:T(1,128)} %bitcast.29, bf16[2048,1536]{1,0:T(8,128)(2,1)} %refs_4_.3, f32[1,1536]{1,0:T(1,128)} %broadcast_in_dim.58.refs_5_, ...), custom_call_target="tpu_custom_call" | custom-call | flops 8999999488 | bytes 20000000 | tf_op jit(solution)/shard_map/second_pass/pallas_call | solution.py:464
  211.2 1.7 copy.41
  (4 shorter events, 0.0 us)
Async XLA Ops:
  0.0 20.5 %copy-start = (bf16[4,2048,16]{1,2,0:T(8,128)(2,1)S(1)}, bf16[4,2048,16]{1,2,0:T(8,128)(2,1)}, u32[]{:S(2)}) copy-start(bf16[4,2048,16]{1,2,0:T(8,128)(2,1)} %param.27) | copy-start | bytes 786436

commit v4 on v3

--- a/solution.py
+++ b/solution.py
@@ -171,9 +171,9 @@
     loads[0].wait()
     low = jnp.dot(normed[...], ad_ref[...], preferred_element_type=F32).astype(BF16)
 
-    @pl.loop(0, wq.shape[1] // 256)
+    @pl.loop(0, wq.shape[1] // 512)
     def _(tile):
-        cols = columns(tile, 256)
+        cols = columns(tile, 512)
         joined = jnp.dot(normed[...], wq[:, cols], preferred_element_type=F32)
         joined = joined + jnp.dot(low, au_ref[:, cols], preferred_element_type=F32)
         qkv[:, cols] = (joined + bq_ref[:, cols]).astype(BF16)
@@ -243,9 +243,9 @@
 
     loads[3].wait()
 
-    @pl.loop(0, wo.shape[1] // 256)
+    @pl.loop(0, wo.shape[1] // 512)
     def _(tile):
-        cols = columns(tile, 256)
+        cols = columns(tile, 512)
         part_a[:, cols] = jnp.dot(ctx[...], wo[:, cols], preferred_element_type=F32).astype(BF16)
 
     piece_rows = 16
@@ -320,17 +320,17 @@
 
     loads[4].wait()
 
-    @pl.loop(0, wu.shape[1] // 256)
+    @pl.loop(0, wu.shape[1] // 512)
     def _(tile):
-        cols = columns(tile, 256)
+        cols = columns(tile, 512)
         inner = jnp.dot(post[...], wu[:, cols], preferred_element_type=F32) + bu_ref[:, cols]
         hid[:, cols] = jax.nn.gelu(inner, approximate=True).astype(BF16)
 
     loads[5].wait()
 
-    @pl.loop(0, wd.shape[1] // 256)
+    @pl.loop(0, wd.shape[1] // 512)
     def _(tile):
-        cols = columns(tile, 256)
+        cols = columns(tile, 512)
         part_b[:, cols] = jnp.dot(hid[...], wd[:, cols], preferred_element_type=F32).astype(BF16)
 
     def sum_copy(landing, index, step):

time: 213 us -> 211 us (level)
  no operation moved by 1% of the time
where the time goes in v4:
time: 211 us
  Pallas kernels  180 us (85%)
  local copies, waits for them, and re-layouts  14.6 us (7%)
  blocking collectives  10.5 us (5%)
  other arithmetic  3.11 us (1%)
  between operations  2.69 us (1%)
    pallas_call x2, Pallas kernels, layer_call(): pl.pallas_call(functools.partial(layer_kernel, n, n_req, rows, heads, emb...  180 us
    all_gather x1, blocking collectives, shards(): all_ids = lax.all_gather(replacement_token_index, 'req', axis=0)  10.5 us
    gather x1, local copies, waits for them, and re-layouts, shards(): found = word_embedding_table.at[wanted].get(mode='promise_in_bounds')  7.01 us

profile of v4, /device:TPU:0, one launch (start us, length us, event | category | flops | bytes accessed | tf_op | source)
XLA Modules:
  0.0 210.9 jit_solution(428616202056017796)
XLA Ops:
  0.0 0.0 copy-start
  0.7 1.3 fusion.9
  3.9 0.7 broadcast_divide_fusion
  4.6 0.2 convert_reduce_fusion
  4.8 0.7 multiply_add_fusion
  5.5 1.3 broadcast_in_dim.58.refs_5_
  6.8 10.5 %all-gather.1 = s32[8,1,256]{2,1,0:T(1,128)S(1)} all-gather(s32[1,1,256]{2,1,0:T(1,128)} %bitcast.19), channel_id=2, replica_groups=mesh['req'=8,'tp'=4] {'req'}, dimensions={0}, use_global_device_ids=true | all-gather | bytes 9216 | tf_op jit(solution)/shard_map/all_gather | solution.py:538
  17.3 0.2 fusion
  17.4 0.2 select_reduce_fusion
  17.6 0.1 reshape.35
  17.8 1.3 copy.35.refs_20_
  19.1 1.4 dynamic-slice_bitcast_fusion.refs_7_
  20.5 0.0 copy-done
  20.5 0.8 copy.34.refs_19_
  21.3 1.0 copy.32
  22.3 7.0 %gather_fusion = bf16[768,512]{1,0:T(8,128)(2,1)} fusion(bf16[6272,512]{1,0:T(8,128)(2,1)} %param.43, s32[1024]{0:T(1024)S(1)} %pad_clamp_fusion), kind=kCustom, calls=%fused_computation | custom fusion | bytes 1575936 | tf_op jit(solution)/shard_map/gather | solution.py:546
  29.3 102.7 %first_pass.1.refs_1_ = bf16[64,2048]{1,0:T(8,128)(2,1)} custom-call(s32[1]{0:T(128)S(6)} %copy.40.refs_0_, bf16[64,2048]{1,0:T(8,128)(2,1)} %refs_1_.1, f32[1,2048]{1,0:T(1,128)} %bitcast.26, f32[1,2048]{1,0:T(1,128)} %bitcast.28, bf16[2048,1536]{1,0:T(8,128)(2,1)} %refs_4_.3, f32[1,1536]{1,0:T(1,128)} %broadcast_in_dim.58.refs_5_, ...), custom_call_target="tpu_custom_call" | custom-call | flops 8999999488 | bytes 20000000 | tf_op jit(solution)/shard_map/first_pass/pallas_call | solution.py:464
  132.0 77.2 %second_pass.1 = bf16[64,2048]{1,0:T(8,128)(2,1)} custom-call(s32[1]{0:T(128)S(6)} %copy.40.refs_0_, bf16[64,2048]{1,0:T(8,128)(2,1)} %first_pass.1.refs_1_, f32[1,2048]{1,0:T(1,128)} %bitcast.27, f32[1,2048]{1,0:T(1,128)} %bitcast.29, bf16[2048,1536]{1,0:T(8,128)(2,1)} %refs_4_.3, f32[1,1536]{1,0:T(1,128)} %broadcast_in_dim.58.refs_5_, ...), custom_call_target="tpu_custom_call" | custom-call | flops 8999999488 | bytes 20000000 | tf_op jit(solution)/shard_map/second_pass/pallas_call | solution.py:464
  209.2 1.7 copy.41
  (4 shorter events, 0.0 us)
Async XLA Ops:
  0.0 20.5 %copy-start = (bf16[4,2048,16]{1,2,0:T(8,128)(2,1)S(1)}, bf16[4,2048,16]{1,2,0:T(8,128)(2,1)}, u32[]{:S(2)}) copy-start(bf16[4,2048,16]{1,2,0:T(8,128)(2,1)} %param.27) | copy-start | bytes 786436
